TPU v7x, 512 devices: a whole 4x4x16 slice. The times are simulated.
512 devices in a mesh: grp: 8 (over z_lo), ent: 64 (over y, z_hi, x, core).
Axes of the slice: x: 4, y: 4, z: 16 (z_hi: 2, z_lo: 8; z = z_hi * 8 + z_lo), core: 2. Of those that a mesh axis runs over, the one named last changes fastest.
Arguments:
- images: bfloat16 [1536, 1024], P(('grp', 'ent')), may hold values from -256 to 256
- texts: bfloat16 [8, 65536, 1024], P('grp', 'ent'), may hold values from -6 to 6
Outputs:
- prototypes: bfloat16 [8, 65536, 1024], P('grp', 'ent')
- mass: float32 [8, 65536], P('grp', 'ent')
All inputs are finite; a program needn't handle non-finite values.
Results may differ from a plain program's by a relative error of at most 0.0095.
Values may be sent and summed in bfloat16 or wider, within the bound.
No kernel may reach another device: no remote copies, remote signals or barrier semaphores. Data moves between devices by JAX's collectives and lax.ppermute only.
A program may use at most 64 MiB of HBM per device.

v0:
```python
import math

import jax
import jax.numpy as jnp
from jax import lax
from jax.sharding import PartitionSpec as P

sharpness = 3.0


def reduce_stats(local_peak, local_total):
    peak = lax.pmax(local_peak, ("grp", "ent"))
    total = lax.psum(local_total * jnp.exp(local_peak - peak), ("grp", "ent"))
    return (peak, total)


def shards(images, texts):
    width = images.shape[1]
    factor = sharpness / math.sqrt(width)
    slab_rows = texts[0]
    block = slab_rows.shape[0]
    mass_scale = block / images.shape[0]
    gathered = lax.all_gather(images, ("grp", "ent"), axis=0, tiled=True)
    scores = jnp.dot(gathered, slab_rows.T, preferred_element_type=jnp.float32) * factor
    local_peak = jnp.max(scores, axis=1)
    local_total = jnp.sum(jnp.exp(scores - local_peak[:, None]), axis=1)
    peak, total = reduce_stats(local_peak, local_total)
    weights = (jnp.exp(scores - peak[:, None]) / total[:, None]).astype(jnp.bfloat16)
    column = jnp.sum(weights.astype(jnp.float32), axis=0)
    summed = jnp.dot(weights.T, gathered, preferred_element_type=jnp.float32)
    prototypes = (summed / column[:, None]).astype(jnp.bfloat16)
    mass = column * mass_scale
    return (prototypes[None], mass[None])


def solution(mesh):
    return jax.shard_map(
        shards,
        mesh=mesh,
        in_specs=(P(("grp", "ent"), None), P("grp", "ent", None)),
        out_specs=(P("grp", "ent", None), P("grp", "ent")),
        check_vma=False,
    )
```

profile of v0, /device:TPU:1, one launch (start us, length us, event | category | flops | bytes accessed | tf_op | source)
XLA Modules:
  0.0 1063.0 jit_solution(4622242664085582019)
XLA Ops:
  7.2 0.0 copy-start
  7.2 0.0 all-gather.3.cloned.1.call-start
  7.2 0.7 all-gather.3.cloned.1.call-update
  7.9 813.9 %all-gather.3.cloned.1.call-done = bf16[512,3,1024]{2,1,0:T(4,128)(2,1)} async-done(((bf16[1,3,1024]{2,1,0:T(4,128)(2,1)}), bf16[512,3,1024]{2,1,0:T(4,128)(2,1)}) %all-gather.3.cloned.1.call-update) | async-done | bytes 3145744 | tf_op jit(solution)/shard_map/all_gather | solution.py:23
  821.8 8.8 reshape.18
  830.6 0.0 copy-done
  830.6 7.3 multiply_reduce_fusion
  837.9 105.9 %pmax.7 = f32[1536]{0:T(1024)S(1)} all-reduce(f32[1536]{0:T(1024)S(1)} %get-tuple-element.4), channel_id=1, replica_groups=mesh['grp'=8,'ent'=64] {'grp','ent'}, use_global_device_ids=true, to_apply=%region_1.0 | all-reduce | flops 1536 | bytes 12288 | tf_op jit(solution)/shard_map/pmax | solution.py:12
  943.8 3.8 exponential_reduce_fusion
  947.7 99.6 %psum.7 = f32[1536]{0:T(1024)S(1)} all-reduce(f32[1536]{0:T(1024)S(1)} %exponential_multiply_fusion), channel_id=1, replica_groups=mesh['grp'=8,'ent'=64] {'grp','ent'}, use_global_device_ids=true, to_apply=%region_3.0 | all-reduce | flops 1536 | bytes 12288 | tf_op jit(solution)/shard_map/psum | solution.py:13
  1047.3 0.0 copy-start.1
  1047.3 3.7 convert_reduce_fusion
  1051.0 0.6 broadcast_multiply_fusion
  1051.6 0.0 copy-done.1
  1051.6 4.6 fusion.2
  (1 shorter events, 0.0 us)
Async XLA Ops:
  7.2 823.5 %copy-start = (bf16[1,1024,1024]{2,1,0:T(8,128)(2,1)S(1)}, bf16[1,1024,1024]{2,1,0:T(8,128)(2,1)}, u32[]{:S(2)}) copy-start(bf16[1,1024,1024]{2,1,0:T(8,128)(2,1)} %param.3) | copy-start | bytes 6291460
  7.2 814.7 %all-gather.3.cloned.1.call-start = ((), (), s32[]{:S(2)}) async-start(), calls=%async_computation | async-start | bytes 4202496 | tf_op jit(solution)/shard_map/all_gather | solution.py:23
  1047.3 4.4 copy-start.1
Sparse Core Ops, SparseCore 0:
  10.2 811.5 all-gather.2
where the time goes:
time: 1060 us
  waiting for transfers between devices  815 us (77%)
  blocking collectives  205 us (19%)
  between operations  14 us (1%)
  matrix products  11.8 us (1%)
    all_gather x1, waiting for transfers between devices, shards(): gathered = lax.all_gather(images, ('grp', 'ent'), axis=0, tiled=True)  814 us
    pmax x1, blocking collectives, reduce_stats(): peak = lax.pmax(local_peak, ('grp', 'ent'))  106 us
    psum x1, blocking collectives, reduce_stats(): total = lax.psum(local_total * jnp.exp(local_peak - peak), ('grp', 'ent'))  99.6 us
  transfers between devices with their start and end apart: 1, of which 1 were waited for; matrix products, arithmetic and copies ran while one was open for 0% of the time, Pallas kernels for 0%

commit v1 on v0

v1 whole, which is shorter than its diff:
```python
import math

import jax
import jax.numpy as jnp
import numpy as np
from jax import lax
from jax.sharding import Mesh, PartitionSpec as P

sharpness = 3.0

AXES = ("zl", "y", "zh", "x", "c")
SIZES = (8, 4, 2, 4, 2)
Z = ("zh", "zl")
PLANE = ("y", "x")
NEAR = ("y", "x", "c")


def count(axes):
    return math.prod(SIZES[AXES.index(a)] for a in axes)


def spread(block, axes):
    n = count(axes)
    copies = lax.optimization_barrier(jnp.broadcast_to(block[None], (n,) + block.shape))
    return lax.all_to_all(copies, axes, 0, 0, tiled=True)


def merge(lse, axes):
    got = spread(lse, axes)
    top = jnp.max(got, axis=0)
    return top + jnp.log(jnp.sum(jnp.exp(got - top[None]), axis=0))


def shards(images, texts):
    rows, width = images.shape
    factor = sharpness / math.sqrt(width)
    slab_rows = texts[0]
    block = slab_rows.shape[0]
    n = count(AXES) * rows
    mass_scale = block * count(AXES) / n
    mine = spread(images.reshape(-1, 128), Z).reshape(-1, 128)
    mine = spread(mine, PLANE).reshape(-1, width)
    other = lax.ppermute(mine, "c", [(0, 1), (1, 0)])
    gathered = jnp.concatenate([mine, other], axis=0)
    scores = jnp.dot(slab_rows, gathered.T, preferred_element_type=jnp.float32) * factor
    local_peak = jnp.max(scores, axis=0)
    local_total = jnp.sum(jnp.exp(scores - local_peak[None]), axis=0)
    lse = (local_peak + jnp.log(local_total)).reshape(2, -1, 128)
    core = lax.axis_index("c")
    lse = jnp.where(core == 0, lse, lse[::-1])
    lse = merge(merge(lse, NEAR), Z)
    lse = jnp.where(core == 0, lse, lse[::-1]).reshape(-1)
    weights = jnp.exp(scores - lse[None]).astype(jnp.bfloat16)
    column = jnp.sum(weights.astype(jnp.float32), axis=1)
    summed = jnp.dot(weights, gathered, preferred_element_type=jnp.float32)
    prototypes = (summed / column[:, None]).astype(jnp.bfloat16)
    mass = column * mass_scale
    return (prototypes[None], mass[None])


def solution(mesh):
    fine = Mesh(np.asarray(mesh.devices).reshape(SIZES), AXES)
    grp, ent = AXES[:1], AXES[1:]
    return jax.shard_map(
        shards,
        mesh=fine,
        in_specs=(P(AXES, None), P(grp, ent, None)),
        out_specs=(P(grp, ent, None), P(grp, ent)),
        check_vma=False,
    )
```

time: 1060 us -> 119 us (0.11)
  waiting for transfers between devices: 815 us -> 1.82 us
  blocking collectives: 205 us -> 81.8 us
  between operations: 14 us -> 0.78 us
    all_gather x1 -> x0, waiting for transfers between devices: 814 us -> none  [shards(): gathered = lax.all_gather(images, ('grp', 'ent'), axis=0, tiled=True)]
    pmax x1 -> x0, blocking collectives: 106 us -> none  [reduce_stats(): peak = lax.pmax(local_peak, ('grp', 'ent'))]
    psum x1 -> x0, blocking collectives: 99.6 us -> none  [reduce_stats(): total = lax.psum(local_total * jnp.exp(local_peak - peak), ('grp', 'ent'))]
    all_to_all x0 -> x4, blocking collectives: none -> 81.8 us  [spread(): return lax.all_to_all(copies, axes, 0, 0, tiled=True)]
  transfers between devices with their start and end apart: 1 -> 1, of which waited for: 1 -> 1; matrix products, arithmetic and copies ran while one was open for 0% -> 1% of each run, Pallas kernels for 0% -> 0%
where the time goes in v1:
time: 119 us; the launch traced here: 118 us
  blocking collectives  81.8 us (69%)
  local copies, waits for them, and re-layouts  11.3 us (9%)
  matrix products  10 us (8%)
  other arithmetic  6.1 us (5%)
  starting transfers between devices  6.05 us (5%)
  waiting for transfers between devices  1.82 us (2%)
    all_to_all x4, blocking collectives, spread(): return lax.all_to_all(copies, axes, 0, 0, tiled=True)  81.8 us
    dot_general x1, matrix products, shards(): summed = jnp.dot(weights, gathered, preferred_element_type=jnp.float32)  6.54 us
    ppermute x1, starting transfers between devices, shards(): other = lax.ppermute(mine, 'c', [(0, 1), (1, 0)])  6.05 us
    unnamed x9, local copies, waits for them, and re-layouts  4.76 us
    reduce_sum x1, other arithmetic, shards(): column = jnp.sum(weights.astype(jnp.float32), axis=1)  4.03 us
    reshape x1, local copies, waits for them, and re-layouts, shards(): mine = spread(mine, PLANE).reshape(-1, width)  3.68 us
    dot_general x1, matrix products, shards(): jnp.dot(slab_rows, gathered.T, preferred_element_type=jnp.float32) * factor  3.47 us
  transfers between devices with their start and end apart: 1, of which 1 were waited for; matrix products, arithmetic and copies ran while one was open for 1% of the time, Pallas kernels for 0%

profile of v1, /device:TPU:1, one launch (start us, length us, event | category | flops | bytes accessed | tf_op | source)
XLA Modules:
  0.0 117.8 jit_solution(10731272893851201978)
XLA Ops:
  0.6 0.0 copy-start
  0.6 0.9 broadcast_in_dim.14
  1.5 27.4 %all_to_all.20 = bf16[16,24,128]{2,1,0:T(8,128)(2,1)S(1)} all-to-all(bf16[16,24,128]{2,1,0:T(8,128)(2,1)S(1)} %broadcast_in_dim.15), channel_id=1, replica_groups=mesh['zl'=8,'y'=4,'zh'=2,'x'=4,'c'=2] {'zh','zl'}, dimensions={0} | all-to-all | bytes 196608 | tf_op jit(solution)/shard_map/all_to_all | solution.py:25
  28.9 0.3 broadcast_in_dim.17
  29.2 26.4 %all_to_all.21 = bf16[16,384,128]{2,1,0:T(8,128)(2,1)} all-to-all(bf16[16,384,128]{2,1,0:T(8,128)(2,1)S(1)} %broadcast_in_dim.17), channel_id=1, replica_groups=mesh['zl'=8,'y'=4,'zh'=2,'x'=4,'c'=2] {'y','x'}, dimensions={0} | all-to-all | bytes 3145728 | tf_op jit(solution)/shard_map/all_to_all | solution.py:25
  55.6 3.7 %reshape.35 = bf16[768,1024]{1,0:T(8,128)(2,1)} reshape(bf16[16,384,128]{2,1,0:T(8,128)(2,1)} %all_to_all.21) | data formatting | bytes 3145728 | tf_op jit(solution)/shard_map/reshape | solution.py:42
  59.3 6.1 %collective-permute-start = (bf16[768,1024]{1,0:T(8,128)(2,1)}, bf16[768,1024]{1,0:T(8,128)(2,1)}, u32[]{:S(2)}, u32[]{:S(2)}) collective-permute-start(bf16[768,1024]{1,0:T(8,128)(2,1)} %reshape.35), channel_id=1, source_target_pairs={{0,1},{1,0},{2,3},{3,2},{4,5},{5,4},{6,7},{7,6},{8,9},{9,8},{10,11... | collective-permute-start | bytes 4718600 | tf_op jit(solution)/shard_map/ppermute | solution.py:43
  65.3 1.5 %constant_dynamic-update-slice_fusion.1 = bf16[1536,1024]{1,0:T(8,128)(2,1)S(1)} fusion(bf16[768,1024]{1,0:T(8,128)(2,1)} %reshape.35), kind=kLoop, calls=%fused_computation.12 | loop fusion | bytes 3145728
  66.9 1.8 %collective-permute-done = bf16[768,1024]{1,0:T(8,128)(2,1)} collective-permute-done((bf16[768,1024]{1,0:T(8,128)(2,1)}, bf16[768,1024]{1,0:T(8,128)(2,1)}, u32[]{:S(2)}, u32[]{:S(2)}) %collective-permute-start) | collective-permute-done | bytes 1572896 | tf_op jit(solution)/shard_map/ppermute | solution.py:43
  68.7 1.5 %constant_dynamic-update-slice_fusion = bf16[1536,1024]{1,0:T(8,128)(2,1)S(1)} fusion(bf16[1536,1024]{1,0:T(8,128)(2,1)S(1)} %constant_dynamic-update-slice_fusion.1, bf16[768,1024]{1,0:T(8,128)(2,1)} %collective-permute-done), kind=kLoop, calls=%fused_computation.11 | loop fusion | bytes 3145728 | tf_op jit(solution)/shard_map/concatenate | solution.py:44
  70.2 0.0 copy-done
  70.2 0.0 copy-start.3
  70.2 3.5 %multiply_reduce_fusion = (f32[1536]{0:T(1024)S(1)}, f32[1536,1024]{0,1:T(8,128)S(1)}) fusion(bf16[1536,1024]{1,0:T(8,128)(2,1)S(1)} %constant_dynamic-update-slice_fusion, bf16[1,1024,1024]{2,1,0:T(8,128)(2,1)S(1)} %copy-done), kind=kOutput, calls=%fused_computation.3 | convolution fusion | flops 3224369664 | bytes 11540480 | tf_op jit(solution)/shard_map/dot_general | solution.py:45
  73.7 0.0 copy-done.3
  73.7 0.0 copy-start.1
  73.7 2.7 %copy-done.1 = f32[1536,1024]{0,1:T(8,128)} copy-done((f32[1536,1024]{0,1:T(8,128)}, f32[1536,1024]{0,1:T(8,128)S(1)}, u32[]{:S(2)}) %copy-start.1) | copy-done | bytes 6291480
  76.4 1.1 exponential_reduce_fusion
  77.5 0.1 broadcast_in_dim.18
  77.6 11.5 %all_to_all.22 = f32[32,2,6,128]{3,1,2,0:T(2,128)S(1)} all-to-all(f32[32,2,6,128]{3,1,2,0:T(2,128)S(1)} %broadcast_in_dim.18), channel_id=1, replica_groups=mesh['zl'=8,'y'=4,'zh'=2,'x'=4,'c'=2] {'y','x','c'}, dimensions={0} | all-to-all | bytes 393216 | tf_op jit(solution)/shard_map/all_to_all | solution.py:25
  89.1 0.1 reduce_max.28
  89.2 0.2 exponential_reduce_fusion.1
  89.4 16.5 %all_to_all.23 = f32[16,2,6,128]{3,1,2,0:T(2,128)S(1)} all-to-all(f32[16,2,6,128]{3,1,2,0:T(2,128)S(1)} %broadcast_in_dim.19), channel_id=1, replica_groups=mesh['zl'=8,'y'=4,'zh'=2,'x'=4,'c'=2] {'zh','zl'}, dimensions={0} | all-to-all | bytes 196608 | tf_op jit(solution)/shard_map/all_to_all | solution.py:25
  106.0 0.1 exponential_reduce_fusion.2
  106.1 0.0 copy-start.2
  106.1 4.0 %convert_reduce_fusion = f32[1024]{0:T(1024)S(1)} fusion(f32[1536]{0:T(1024)S(1)} %sub.42, f32[1536,1024]{0,1:T(8,128)} %copy-done.1), kind=kLoop, calls=%fused_computation | loop fusion | flops 7863296 | bytes 6301696 | tf_op jit(solution)/shard_map/reduce_sum | solution.py:54
  110.2 0.6 copy-done.2
  110.7 6.5 %fusion.2 = bf16[1,1024,1024]{2,1,0:T(8,128)(2,1)} fusion(f32[1024]{0:T(1024)S(1)} %convert_reduce_fusion, bf16[1536,1024]{1,0:T(8,128)(2,1)} %copy-done.3, f32[1536,1024]{0,1:T(8,128)S(1)} %copy-done.2, f32[1536]{0:T(1024)S(1)} %sub.42), kind=kOutput, calls=%fused_computation.7 | convolution fusion | flops 3228041216 | bytes 11544576 | tf_op jit(solution)/shard_map/dot_general | solution.py:55
  117.3 0.6 broadcast_multiply_fusion
  (14 shorter events, 0.2 us)
Async XLA Ops:
  0.6 69.6 %copy-start = (bf16[1,1024,1024]{2,1,0:T(8,128)(2,1)S(1)}, bf16[1,1024,1024]{2,1,0:T(8,128)(2,1)}, u32[]{:S(2)}) copy-start(bf16[1,1024,1024]{2,1,0:T(8,128)(2,1)} %param.3) | copy-start | bytes 6291460
  59.3 9.4 %collective-permute-start = (bf16[768,1024]{1,0:T(8,128)(2,1)}, bf16[768,1024]{1,0:T(8,128)(2,1)}, u32[]{:S(2)}, u32[]{:S(2)}) collective-permute-start(bf16[768,1024]{1,0:T(8,128)(2,1)} %reshape.35), channel_id=1, source_target_pairs={{0,1},{1,0},{2,3},{3,2},{4,5},{5,4},{6,7},{7,6},{8,9},{9,8},{10,11... | collective-permute-start | bytes 4718600 | tf_op jit(solution)/shard_map/ppermute | solution.py:43
  70.2 3.5 %copy-start.3 = (bf16[1536,1024]{1,0:T(8,128)(2,1)}, bf16[1536,1024]{1,0:T(8,128)(2,1)S(1)}, u32[]{:S(2)}) copy-start(bf16[1536,1024]{1,0:T(8,128)(2,1)S(1)} %constant_dynamic-update-slice_fusion) | copy-start | bytes 9437188
  73.7 2.7 %copy-start.1 = (f32[1536,1024]{0,1:T(8,128)}, f32[1536,1024]{0,1:T(8,128)S(1)}, u32[]{:S(2)}) copy-start(f32[1536,1024]{0,1:T(8,128)S(1)} %get-tuple-element.3) | copy-start | bytes 18874372
  106.1 4.6 %copy-start.2 = (f32[1536,1024]{0,1:T(8,128)S(1)}, f32[1536,1024]{0,1:T(8,128)}, u32[]{:S(2)}) copy-start(f32[1536,1024]{0,1:T(8,128)} %copy-done.1) | copy-start | bytes 18874372

commit v2 on v1

v2 whole, which is shorter than its diff:
```python
import functools
import math

import jax
import jax.numpy as jnp
import numpy as np
from jax import lax
from jax.experimental import pallas as pl
from jax.experimental.pallas import tpu as pltpu
from jax.sharding import Mesh, PartitionSpec as P

sharpness = 3.0

AXES = ("zl", "y", "zh", "x", "c")
SIZES = (8, 4, 2, 4, 2)
Z = ("zh", "zl")
PLANE = ("y", "x")
NEAR = ("y", "x", "c")
WHOLE = pl.BlockSpec(memory_space=pltpu.VMEM)
PARAMS = pltpu.CompilerParams(vmem_limit_bytes=48 << 20)


def count(axes):
    return math.prod(SIZES[AXES.index(a)] for a in axes)


def spread(block, axes):
    n = count(axes)
    copies = lax.optimization_barrier(jnp.broadcast_to(block[None], (n,) + block.shape))
    return lax.all_to_all(copies, axes, 0, 0, tiled=True)


def merge(lse, axes):
    got = spread(lse, axes)
    top = jnp.max(got, axis=0)
    return top + jnp.log(jnp.sum(jnp.exp(got - top[None]), axis=0))


def scores_kernel(factor, texts, images, shares, stats):
    dots = lax.dot_general(texts[...], images[...], (((1,), (1,)), ((), ())), preferred_element_type=jnp.float32)
    top = jnp.max(dots, axis=0, keepdims=True)
    parts = jnp.exp2((dots - top) * (factor * math.log2(math.e)))
    shares[...] = parts.astype(jnp.bfloat16)
    stats[0:1] = top * factor
    stats[1:2] = top * factor + jnp.log(jnp.sum(parts, axis=0, keepdims=True))


def scores(texts, images, factor):
    (entries, width), n = texts.shape, images.shape[0]
    return pl.pallas_call(
        functools.partial(scores_kernel, factor),
        out_shape=[jax.ShapeDtypeStruct((entries, n), jnp.bfloat16), jax.ShapeDtypeStruct((2, n), jnp.float32)],
        in_specs=[WHOLE] * 2,
        out_specs=[WHOLE] * 2,
        compiler_params=PARAMS,
        name="scores",
        cost_estimate=pl.CostEstimate(flops=2 * entries * width * n, bytes_accessed=2 * (entries * width + n * width + entries * n), transcendentals=entries * n),
    )(texts, images)


def prototypes_kernel(mass_scale, shares_a, shares_b, scale_a, scale_b, images_a, images_b, out, mass):
    weights_a = (shares_a[...].astype(jnp.float32) * scale_a[...]).astype(jnp.bfloat16)
    weights_b = (shares_b[...].astype(jnp.float32) * scale_b[...]).astype(jnp.bfloat16)
    lanes = None
    for weights in (weights_a, weights_b):
        for j in range(0, weights.shape[1], 128):
            part = weights[:, j : j + 128].astype(jnp.float32)
            lanes = part if lanes is None else lanes + part
    summed = jnp.dot(weights_a, images_a[...], preferred_element_type=jnp.float32)
    summed += jnp.dot(weights_b, images_b[...], preferred_element_type=jnp.float32)
    out[0] = (summed / jnp.sum(lanes, axis=1, keepdims=True)).astype(jnp.bfloat16)
    mass[...] = jnp.sum(lanes.T, axis=0, keepdims=True) * mass_scale


def prototypes(shares, scales, images, mass_scale, steps=2):
    (entries, n), width = shares[0].shape, images[0].shape[1]
    rows = entries // steps
    return pl.pallas_call(
        functools.partial(prototypes_kernel, mass_scale),
        grid=(steps,),
        out_shape=[jax.ShapeDtypeStruct((1, entries, width), jnp.bfloat16), jax.ShapeDtypeStruct((1, entries), jnp.float32)],
        in_specs=[pl.BlockSpec((rows, n), lambda i: (i, 0))] * 2 + [WHOLE] * 4,
        out_specs=[pl.BlockSpec((1, rows, width), lambda i: (0, i, 0)), pl.BlockSpec((1, rows), lambda i: (0, i))],
        compiler_params=PARAMS,
        name="prototypes",
        cost_estimate=pl.CostEstimate(flops=4 * entries * width * n, bytes_accessed=4 * (entries * width + n * width + entries * n), transcendentals=0),
    )(*shares, *scales, *images)


def shards(images, texts):
    rows, width = images.shape
    factor = sharpness / math.sqrt(width)
    slab_rows = texts[0]
    block = slab_rows.shape[0]
    n = count(AXES) * rows
    mass_scale = block * count(AXES) / n
    line = spread(images.reshape(-1, 128), Z).reshape(-1, width)
    mine = spread(line, PLANE).reshape(-1, width)
    other = lax.ppermute(mine, "c", [(0, 1), (1, 0)])
    shares_a, stats_a = scores(slab_rows, mine, factor)
    shares_b, stats_b = scores(slab_rows, other, factor)
    core = lax.axis_index("c")
    lse_a, lse_b = stats_a[1].reshape(1, -1, 128), stats_b[1].reshape(1, -1, 128)
    lse = jnp.concatenate([jnp.where(core == 0, lse_a, lse_b), jnp.where(core == 0, lse_b, lse_a)])
    lse = merge(merge(lse, NEAR), Z).reshape(2, 1, -1)
    scale_a = jnp.exp(stats_a[0:1] - jnp.where(core == 0, lse[0], lse[1]))
    scale_b = jnp.exp(stats_b[0:1] - jnp.where(core == 0, lse[1], lse[0]))
    return prototypes((shares_a, shares_b), (scale_a, scale_b), (mine, other), mass_scale)


def solution(mesh):
    fine = Mesh(np.asarray(mesh.devices).reshape(SIZES), AXES)
    grp, ent = AXES[:1], AXES[1:]
    return jax.shard_map(
        shards,
        mesh=fine,
        in_specs=(P(AXES, None), P(grp, ent, None)),
        out_specs=(P(grp, ent, None), P(grp, ent)),
        check_vma=False,
    )
```

time: 119 us -> 106 us (0.89)
  Pallas kernels: 0 us -> 10.9 us
  matrix products: 10 us -> 0 us
  local copies, waits for them, and re-layouts: 11.3 us -> 5.19 us
  other arithmetic: 6.1 us -> 0.44 us
  waiting for transfers between devices: 1.82 us -> 0.01 us
    pallas_call x0 -> x3, Pallas kernels: none -> 10.9 us  [the longest x1 6.09 us: prototypes(): pl.pallas_call(functools.partial(prototypes_kernel, mass_scale), grid=(st...]
    dot_general x2 -> x0, matrix products: 10 us -> none  [the longest x1 6.54 us: shards(): summed = jnp.dot(weights, gathered, preferred_element_type=jnp.float32)]
    reduce_sum x2 -> x0, other arithmetic: 5.09 us -> none  [the longest x1 4.03 us: shards(): column = jnp.sum(weights.astype(jnp.float32), axis=1)]
    reshape x1 -> x0, local copies, waits for them, and re-layouts: 3.68 us -> none  [shards(): mine = spread(mine, PLANE).reshape(-1, width)]
    ppermute x1, waiting for transfers between devices: 1.82 us -> 0.01 us  [shards(): other = lax.ppermute(mine, 'c', [(0, 1), (1, 0)])]
    concatenate x1, local copies, waits for them, and re-layouts: 1.53 us -> 0.01 us  [shards(): jnp.concatenate([jnp.where(core == 0, lse_a, lse_b), jnp.where(core == 0,...]
    unnamed x9 -> x12, local copies, waits for them, and re-layouts: 4.76 us -> 4.14 us
  transfers between devices with their start and end apart: 1 -> 1, of which waited for: 1 -> 0; matrix products, arithmetic and copies ran while one was open for 1% -> 0% of each run, Pallas kernels for 0% -> 2%
where the time goes in v2:
time: 106 us; the launch traced here: 105 us
  blocking collectives  81.6 us (77%)
  Pallas kernels  10.9 us (10%)
  starting transfers between devices  6.05 us (6%)
  local copies, waits for them, and re-layouts  5.19 us (5%)
    all_to_all x4, blocking collectives, spread(): return lax.all_to_all(copies, axes, 0, 0, tiled=True)  81.6 us
    pallas_call x1, Pallas kernels, prototypes(): pl.pallas_call(functools.partial(prototypes_kernel, mass_scale), grid=(st...  6.09 us
    ppermute x1, starting transfers between devices, shards(): other = lax.ppermute(mine, 'c', [(0, 1), (1, 0)])  6.05 us
    pallas_call x2, Pallas kernels, scores(): pl.pallas_call(functools.partial(scores_kernel, factor), out_shape=[jax.S...  4.8 us
    unnamed x12, local copies, waits for them, and re-layouts  4.14 us
  transfers between devices with their start and end apart: 1, of which 0 were waited for; matrix products, arithmetic and copies ran while one was open for 0% of the time, Pallas kernels for 2%

profile of v2, /device:TPU:1, one launch (start us, length us, event | category | flops | bytes accessed | tf_op | source)
XLA Modules:
  0.0 104.9 jit_solution(13663743959190255616)
XLA Ops:
  0.6 0.7 broadcast_in_dim.12
  1.4 27.4 %all_to_all.20 = bf16[16,24,128]{2,1,0:T(8,128)(2,1)S(1)} all-to-all(bf16[16,24,128]{2,1,0:T(8,128)(2,1)S(1)} %broadcast_in_dim.13), channel_id=1, replica_groups=mesh['zl'=8,'y'=4,'zh'=2,'x'=4,'c'=2] {'zh','zl'}, dimensions={0} | all-to-all | bytes 196608 | tf_op jit(solution)/shard_map/all_to_all | solution.py:30
  28.8 0.2 broadcast_in_dim.15
  29.0 26.3 %all_to_all.21 = bf16[16,48,1024]{2,1,0:T(8,128)(2,1)S(1)} all-to-all(bf16[16,48,1024]{2,1,0:T(8,128)(2,1)S(1)} %broadcast_in_dim.15), channel_id=1, replica_groups=mesh['zl'=8,'y'=4,'zh'=2,'x'=4,'c'=2] {'y','x'}, dimensions={0} | all-to-all | bytes 3145728 | tf_op jit(solution)/shard_map/all_to_all | solution.py:30
  55.3 6.1 %collective-permute-start = (bf16[768,1024]{1,0:T(8,128)(2,1)S(1)}, bf16[768,1024]{1,0:T(8,128)(2,1)S(1)}, u32[]{:S(2)}, u32[]{:S(2)}) collective-permute-start(bf16[768,1024]{1,0:T(8,128)(2,1)S(1)} %bitcast.16), channel_id=1, source_target_pairs={{0,1},{1,0},{2,3},{3,2},{4,5},{5,4},{6,7},{7,6},{8,9},{9,8},{10,11... | collective-permute-start | bytes 4718600 | tf_op jit(solution)/shard_map/ppermute | solution.py:99
  61.3 0.0 copy-start
  61.3 1.6 %copy-done = bf16[1,1024,1024]{2,1,0:T(8,128)(2,1)S(1)} copy-done((bf16[1,1024,1024]{2,1,0:T(8,128)(2,1)S(1)}, bf16[1,1024,1024]{2,1,0:T(8,128)(2,1)}, u32[]{:S(2)}) %copy-start) | copy-done | bytes 2097176
  62.9 2.4 %scores.2 = (bf16[1024,768]{1,0:T(8,128)(2,1)S(1)}, f32[2,768]{1,0:T(2,128)S(1)}) custom-call(bf16[1024,1024]{1,0:T(8,128)(2,1)S(1)} %bitcast.19, bf16[768,1024]{1,0:T(8,128)(2,1)S(1)} %bitcast.17), custom_call_target="tpu_custom_call" | custom-call | flops 1610612736 | bytes 5242880 | tf_op jit(solution)/shard_map/scores/pallas_call | solution.py:50
  65.3 0.0 copy-start.2
  65.3 0.0 collective-permute-done.images.images_b
  65.3 0.0 copy-start.1
  65.4 2.4 %scores.3 = (bf16[1024,768]{1,0:T(8,128)(2,1)S(1)}, f32[2,768]{1,0:T(2,128)S(1)}) custom-call(bf16[1024,1024]{1,0:T(8,128)(2,1)S(1)} %bitcast.20, bf16[768,1024]{1,0:T(8,128)(2,1)S(1)} %collective-permute-done.images.images_b), custom_call_target="tpu_custom_call" | custom-call | flops 1610612736 | bytes 5242880 | tf_op jit(solution)/shard_map/scores/pallas_call | solution.py:50
  67.8 0.0 copy-done.2
  67.8 0.0 copy-done.1
  67.8 0.0 copy-start.4
  67.8 1.1 %copy-done.4 = bf16[1024,768]{1,0:T(8,128)(2,1)} copy-done((bf16[1024,768]{1,0:T(8,128)(2,1)}, bf16[1024,768]{1,0:T(8,128)(2,1)S(1)}, u32[]{:S(2)}) %copy-start.4) | copy-done | bytes 1572888
  68.9 0.0 copy-start.3
  69.0 0.1 broadcast_in_dim.32
  69.0 11.4 %all_to_all.22 = f32[32,2,6,128]{3,1,2,0:T(2,128)S(1)} all-to-all(f32[32,2,6,128]{3,1,2,0:T(2,128)S(1)} %broadcast_in_dim.32), channel_id=1, replica_groups=mesh['zl'=8,'y'=4,'zh'=2,'x'=4,'c'=2] {'y','x','c'}, dimensions={0} | all-to-all | bytes 393216 | tf_op jit(solution)/shard_map/all_to_all | solution.py:30
  80.4 0.1 reduce_max.18
  80.5 0.2 exponential_reduce_fusion
  80.7 16.5 %all_to_all.23 = f32[16,2,6,128]{3,1,2,0:T(2,128)S(1)} all-to-all(f32[16,2,6,128]{3,1,2,0:T(2,128)S(1)} %broadcast_in_dim.33), channel_id=1, replica_groups=mesh['zl'=8,'y'=4,'zh'=2,'x'=4,'c'=2] {'zh','zl'}, dimensions={0} | all-to-all | bytes 196608 | tf_op jit(solution)/shard_map/all_to_all | solution.py:30
  97.3 0.1 exponential_reduce_fusion.1
  97.4 0.0 copy-done.3
  97.4 0.0 copy-start.5
  97.4 1.4 %copy-done.5 = bf16[1024,768]{1,0:T(8,128)(2,1)S(1)} copy-done((bf16[1024,768]{1,0:T(8,128)(2,1)S(1)}, bf16[1024,768]{1,0:T(8,128)(2,1)}, u32[]{:S(2)}) %copy-start.5) | copy-done | bytes 1572888
  98.8 6.1 %prototypes.1 = (bf16[1,1024,1024]{2,1,0:T(8,128)(2,1)}, f32[1,1024]{1,0:T(1,128)}) custom-call(bf16[1024,768]{1,0:T(8,128)(2,1)S(1)} %copy-done.3, bf16[1024,768]{1,0:T(8,128)(2,1)S(1)} %copy-done.5, f32[1,768]{1,0:T(1,128)S(1)} %get-tuple-element.13.scale_a, f32[1,768]{1,0:T(1,128)S(1)} %get-tuple-element.12.scale_b, bf16[768,1024]{1,0:T(8,128)(2,1)S(1)} %bitcast.18, ...), custom_call_target="tpu_custom_call" | custom-call | flops 3221225472 | bytes 10485760 | tf_op jit(solution)/shard_map/prototypes/pallas_call | solution.py:78
  (10 shorter events, 0.2 us)
Async XLA Ops:
  55.3 10.1 %collective-permute-start = (bf16[768,1024]{1,0:T(8,128)(2,1)S(1)}, bf16[768,1024]{1,0:T(8,128)(2,1)S(1)}, u32[]{:S(2)}, u32[]{:S(2)}) collective-permute-start(bf16[768,1024]{1,0:T(8,128)(2,1)S(1)} %bitcast.16), channel_id=1, source_target_pairs={{0,1},{1,0},{2,3},{3,2},{4,5},{5,4},{6,7},{7,6},{8,9},{9,8},{10,11... | collective-permute-start | bytes 4718600 | tf_op jit(solution)/shard_map/ppermute | solution.py:99
  61.3 1.6 %copy-start = (bf16[1,1024,1024]{2,1,0:T(8,128)(2,1)S(1)}, bf16[1,1024,1024]{2,1,0:T(8,128)(2,1)}, u32[]{:S(2)}) copy-start(bf16[1,1024,1024]{2,1,0:T(8,128)(2,1)} %param.3) | copy-start | bytes 6291460
  65.3 2.4 %copy-start.2 = (bf16[1024,768]{1,0:T(8,128)(2,1)}, bf16[1024,768]{1,0:T(8,128)(2,1)S(1)}, u32[]{:S(2)}) copy-start(bf16[1024,768]{1,0:T(8,128)(2,1)S(1)} %get-tuple-element.6.shares_a) | copy-start | bytes 4718596
  65.3 2.4 %copy-start.1 = (bf16[768,1024]{1,0:T(8,128)(2,1)}, bf16[768,1024]{1,0:T(8,128)(2,1)S(1)}, u32[]{:S(2)}) copy-start(bf16[768,1024]{1,0:T(8,128)(2,1)S(1)} %collective-permute-done.images.images_b) | copy-start | bytes 4718596
  67.8 1.1 %copy-start.4 = (bf16[1024,768]{1,0:T(8,128)(2,1)}, bf16[1024,768]{1,0:T(8,128)(2,1)S(1)}, u32[]{:S(2)}) copy-start(bf16[1024,768]{1,0:T(8,128)(2,1)S(1)} %get-tuple-element.7.shares_b) | copy-start | bytes 4718596
  68.9 28.5 %copy-start.3 = (bf16[1024,768]{1,0:T(8,128)(2,1)S(1)}, bf16[1024,768]{1,0:T(8,128)(2,1)}, u32[]{:S(2)}) copy-start(bf16[1024,768]{1,0:T(8,128)(2,1)} %copy-done.2) | copy-start | bytes 4718596
  97.4 1.4 %copy-start.5 = (bf16[1024,768]{1,0:T(8,128)(2,1)S(1)}, bf16[1024,768]{1,0:T(8,128)(2,1)}, u32[]{:S(2)}) copy-start(bf16[1024,768]{1,0:T(8,128)(2,1)} %copy-done.4) | copy-start | bytes 4718596

commit v3 on v2

v3 whole, which is shorter than its diff:
```python
import functools
import math

import jax
import jax.numpy as jnp
import numpy as np
from jax import lax
from jax.experimental import pallas as pl
from jax.experimental.pallas import tpu as pltpu
from jax.sharding import Mesh, PartitionSpec as P

sharpness = 3.0

AXES = ("zl", "y", "zh", "x", "c")
SIZES = (8, 4, 2, 4, 2)
Z = ("zh", "zl")
PLANE = ("y", "x")
NEAR = ("y", "x", "c")
SWAP = [(0, 1), (1, 0)]
WHOLE = pl.BlockSpec(memory_space=pltpu.VMEM)
bf16, f32 = jnp.bfloat16, jnp.float32
struct = jax.ShapeDtypeStruct


def count(axes):
    return math.prod(SIZES[AXES.index(a)] for a in axes)


def params(mib):
    return pltpu.CompilerParams(vmem_limit_bytes=mib << 20)


def exchange(copies, axes):
    return lax.all_to_all(copies, axes, 0, 0, tiled=True)


def spread(block, axes):
    n = count(axes)
    return exchange(lax.optimization_barrier(jnp.broadcast_to(block[None], (n,) + block.shape)), axes)


def merge(parts):
    top = jnp.max(parts, axis=0)
    return top + jnp.log(jnp.sum(jnp.exp(parts - top[None]), axis=0))


def scores_kernel(factor, texts, images, *refs):
    before, (shares, peak, lse) = refs[:-3], refs[-3:]
    dots = lax.dot_general(texts[...], images[...], (((1,), (1,)), ((), ())), preferred_element_type=f32)
    top = jnp.max(dots, axis=0, keepdims=True)
    parts = jnp.exp2((dots - top) * (factor * math.log2(math.e)))
    shares[...] = parts.astype(bf16)
    peak[...] = top * factor
    here = top * factor + jnp.log(jnp.sum(parts, axis=0, keepdims=True))
    if before:
        core, shape = lax.axis_index("c"), (lse.shape[0], 1) + here.shape
        lse[:, pl.ds(core, 1)] = jnp.broadcast_to(before[0][...], shape)
        lse[:, pl.ds(1 - core, 1)] = jnp.broadcast_to(here, shape)
    else:
        lse[...] = here


def scores(texts, images, factor, before=(), copies=None):
    (entries, width), n = texts.shape, images.shape[0]
    return pl.pallas_call(
        functools.partial(scores_kernel, factor),
        out_shape=[struct((entries, n), bf16), struct((1, n), f32), struct((copies, 2, 1, n) if before else (1, n), f32)],
        in_specs=[WHOLE] * (2 + len(before)),
        out_specs=[WHOLE] * 3,
        compiler_params=params(12),
        name="scores",
        cost_estimate=pl.CostEstimate(flops=2 * entries * width * n, bytes_accessed=2 * (entries * width + n * width + entries * n), transcendentals=entries * n),
    )(texts, images, *before)


def merge_kernel(parts, out):
    out[...] = jnp.broadcast_to(merge(parts[...])[None], out.shape)


def merged(parts, copies):
    return pl.pallas_call(
        merge_kernel,
        out_shape=struct((copies,) + parts.shape[1:], f32),
        in_specs=[WHOLE],
        out_specs=WHOLE,
        compiler_params=params(4),
        name="merge",
        cost_estimate=pl.CostEstimate(flops=4 * parts.size, bytes_accessed=8 * parts.size, transcendentals=parts.size),
    )(parts)


def prototypes_kernel(mass_scale, shares_own, shares_other, parts, peak_own, peak_other, images_own, images_other, out, mass):
    core = lax.axis_index("c")
    lanes = summed = None
    for shares, images, peak, at in ((shares_own, images_own, peak_own, core), (shares_other, images_other, peak_other, 1 - core)):
        scale = jnp.exp(peak[...] - merge(parts[:, pl.ds(at, 1)])[0])
        weights = (shares[...].astype(f32) * scale).astype(bf16)
        for j in range(0, weights.shape[1], 128):
            part = weights[:, j : j + 128].astype(f32)
            lanes = part if lanes is None else lanes + part
        product = jnp.dot(weights, images[...], preferred_element_type=f32)
        summed = product if summed is None else summed + product
    out[0] = (summed * (1.0 / jnp.sum(lanes, axis=1, keepdims=True))).astype(bf16)
    mass[...] = jnp.sum(lanes.T, axis=0, keepdims=True) * mass_scale


def prototypes(shares, parts, peaks, images, mass_scale, steps=2):
    (entries, n), width = shares[0].shape, images[0].shape[1]
    rows = entries // steps
    return pl.pallas_call(
        functools.partial(prototypes_kernel, mass_scale),
        grid=(steps,),
        out_shape=[struct((1, entries, width), bf16), struct((1, entries), f32)],
        in_specs=[pl.BlockSpec((rows, n), lambda i: (i, 0))] * 2 + [WHOLE] * 5,
        out_specs=[pl.BlockSpec((1, rows, width), lambda i: (0, i, 0)), pl.BlockSpec((1, rows), lambda i: (0, i))],
        compiler_params=params(24),
        name="prototypes",
        cost_estimate=pl.CostEstimate(flops=4 * entries * width * n, bytes_accessed=2 * (entries * width + 2 * n * width + 2 * entries * n), transcendentals=0),
    )(*shares, parts, *peaks, *images)


def shards(images, texts):
    rows, width = images.shape
    factor = sharpness / math.sqrt(width)
    own = texts[0]
    mass_scale = own.shape[0] / rows
    line = spread(images.reshape(-1, 128), Z).reshape(-1, width)
    mine = spread(line, PLANE).reshape(-1, width)
    other = lax.ppermute(mine, "c", SWAP)
    shares_own, peak_own, lse = scores(own, mine, factor)
    shares_other, peak_other, lse = scores(own, other, factor, (lse,), count(NEAR))
    parts = exchange(merged(exchange(lse, NEAR), count(Z)), Z)
    return prototypes((shares_own, shares_other), parts, (peak_own, peak_other), (mine, other), mass_scale)


def solution(mesh):
    fine = Mesh(np.asarray(mesh.devices).reshape(SIZES), AXES)
    grp, ent = AXES[:1], AXES[1:]
    return jax.shard_map(
        shards,
        mesh=fine,
        in_specs=(P(AXES, None), P(grp, ent, None)),
        out_specs=(P(grp, ent, None), P(grp, ent)),
        check_vma=False,
    )
```

time: 106 us -> 101 us (0.953)
  local copies, waits for them, and re-layouts: 5.19 us -> 0.97 us
    unnamed x12 -> x2, local copies, waits for them, and re-layouts: 4.14 us -> 0.01 us
    pallas_call x1, Pallas kernels: 6.09 us -> 4.82 us  [prototypes(): pl.pallas_call(functools.partial(prototypes_kernel, mass_scale), grid=(st...]
    pallas_call x2 -> x3, Pallas kernels: 4.8 us -> 5.07 us  [the longest x2 4.83 us: scores(): pl.pallas_call(functools.partial(scores_kernel, factor), out_shape=[struc...]
  transfers between devices with their start and end apart: 1 -> 1, of which waited for: 0 -> 1; matrix products, arithmetic and copies ran while one was open for 0% -> 0% of each run, Pallas kernels for 2% -> 2%
where the time goes in v3:
time: 101 us; the launch traced here: 100 us
  blocking collectives  81.8 us (81%)
  Pallas kernels  9.89 us (10%)
  starting transfers between devices  6.05 us (6%)
    all_to_all x4, blocking collectives, exchange(): return lax.all_to_all(copies, axes, 0, 0, tiled=True)  81.8 us
    ppermute x1, starting transfers between devices, shards(): other = lax.ppermute(mine, 'c', SWAP)  6.05 us
    pallas_call x2, Pallas kernels, scores(): pl.pallas_call(functools.partial(scores_kernel, factor), out_shape=[struc...  4.83 us
    pallas_call x1, Pallas kernels, prototypes(): pl.pallas_call(functools.partial(prototypes_kernel, mass_scale), grid=(st...  4.82 us
  transfers between devices with their start and end apart: 1, of which 1 were waited for; matrix products, arithmetic and copies ran while one was open for 0% of the time, Pallas kernels for 2%

profile of v3, /device:TPU:1, one launch (start us, length us, event | category | flops | bytes accessed | tf_op | source)
XLA Modules:
  0.0 100.0 jit_solution(5249881299963782326)
XLA Ops:
  0.6 0.7 broadcast_in_dim.14
  1.4 27.4 %all_to_all.20 = bf16[16,24,128]{2,1,0:T(8,128)(2,1)S(1)} all-to-all(bf16[16,24,128]{2,1,0:T(8,128)(2,1)S(1)} %broadcast_in_dim.15), channel_id=1, replica_groups=mesh['zl'=8,'y'=4,'zh'=2,'x'=4,'c'=2] {'zh','zl'}, dimensions={0} | all-to-all | bytes 196608 | tf_op jit(solution)/shard_map/all_to_all | solution.py:34
  28.8 0.2 broadcast_in_dim.17
  29.0 0.0 copy-start
  29.0 26.4 %all_to_all.21 = bf16[16,48,1024]{2,1,0:T(8,128)(2,1)S(1)} all-to-all(bf16[16,48,1024]{2,1,0:T(8,128)(2,1)S(1)} %broadcast_in_dim.17), channel_id=1, replica_groups=mesh['zl'=8,'y'=4,'zh'=2,'x'=4,'c'=2] {'y','x'}, dimensions={0} | all-to-all | bytes 3145728 | tf_op jit(solution)/shard_map/all_to_all | solution.py:34
  55.4 6.1 %collective-permute-start = (bf16[768,1024]{1,0:T(8,128)(2,1)S(1)}, bf16[768,1024]{1,0:T(8,128)(2,1)S(1)}, u32[]{:S(2)}, u32[]{:S(2)}) collective-permute-start(bf16[768,1024]{1,0:T(8,128)(2,1)S(1)} %bitcast.2), channel_id=1, source_target_pairs={{0,1},{1,0},{2,3},{3,2},{4,5},{5,4},{6,7},{7,6},{8,9},{9,8},{10,11... | collective-permute-start | bytes 4718600 | tf_op jit(solution)/shard_map/ppermute | solution.py:129
  61.5 0.0 copy-done
  61.5 2.4 %scores.2 = (bf16[1024,768]{1,0:T(8,128)(2,1)S(1)}, f32[1,768]{1,0:T(1,128)S(1)}, f32[1,768]{1,0:T(1,128)S(1)}) custom-call(bf16[1024,1024]{1,0:T(8,128)(2,1)S(1)} %bitcast.5, bf16[768,1024]{1,0:T(8,128)(2,1)S(1)} %bitcast.3), custom_call_target="tpu_custom_call" | custom-call | flops 1610612736 | bytes 5242880 | tf_op jit(solution)/shard_map/scores/pallas_call | solution.py:65
  63.9 0.6 collective-permute-done.images.images_other
  64.5 2.4 %scores.3 = (bf16[1024,768]{1,0:T(8,128)(2,1)S(1)}, f32[1,768]{1,0:T(1,128)S(1)}, f32[32,2,1,768]{3,2,1,0:T(1,128)S(1)}) custom-call(bf16[1024,1024]{1,0:T(8,128)(2,1)S(1)} %bitcast.6, bf16[768,1024]{1,0:T(8,128)(2,1)S(1)} %collective-permute-done.images.images_other, f32[1,768]{1,0:T(1,128)S(1)} %get-tuple-element.9.refs_0_), custom_call_target="tpu_custom_call" | custom-call | flops 1610612736 | bytes 5242880 | tf_op jit(solution)/shard_map/scores/pallas_call | solution.py:65
  66.9 11.5 %all_to_all.22.parts = f32[32,2,1,768]{3,2,1,0:T(1,128)S(1)} all-to-all(f32[32,2,1,768]{3,2,1,0:T(1,128)S(1)} %get-tuple-element.11), channel_id=1, replica_groups=mesh['zl'=8,'y'=4,'zh'=2,'x'=4,'c'=2] {'y','x','c'}, dimensions={0} | all-to-all | bytes 393216 | tf_op jit(solution)/shard_map/all_to_all | solution.py:34
  78.4 0.2 merge.1
  78.7 16.5 %all_to_all.23.parts = f32[16,2,1,768]{3,2,1,0:T(1,128)S(1)} all-to-all(f32[16,2,1,768]{3,2,1,0:T(1,128)S(1)} %merge.1), channel_id=1, replica_groups=mesh['zl'=8,'y'=4,'zh'=2,'x'=4,'c'=2] {'zh','zl'}, dimensions={0} | all-to-all | bytes 196608 | tf_op jit(solution)/shard_map/all_to_all | solution.py:34
  95.2 4.8 %prototypes.1 = (bf16[1,1024,1024]{2,1,0:T(8,128)(2,1)}, f32[1,1024]{1,0:T(1,128)}) custom-call(bf16[1024,768]{1,0:T(8,128)(2,1)S(1)} %get-tuple-element.8.shares_own, bf16[1024,768]{1,0:T(8,128)(2,1)S(1)} %get-tuple-element.10.shares_other, f32[16,2,1,768]{3,2,1,0:T(1,128)S(1)} %all_to_all.23.parts, f32[1,768]{1,0:T(1,128)S(1)} %get-tuple-element.12.peak_own, ...), custom_call_target="tpu_custom_call" | custom-call | flops 3221225472 | bytes 8388608 | tf_op jit(solution)/shard_map/prototypes/pallas_call | solution.py:110
  (2 shorter events, 0.1 us)
Async XLA Ops:
  29.0 32.5 %copy-start = (bf16[1,1024,1024]{2,1,0:T(8,128)(2,1)S(1)}, bf16[1,1024,1024]{2,1,0:T(8,128)(2,1)}, u32[]{:S(2)}) copy-start(bf16[1,1024,1024]{2,1,0:T(8,128)(2,1)} %param.3) | copy-start | bytes 6291460
  55.4 9.1 %collective-permute-start = (bf16[768,1024]{1,0:T(8,128)(2,1)S(1)}, bf16[768,1024]{1,0:T(8,128)(2,1)S(1)}, u32[]{:S(2)}, u32[]{:S(2)}) collective-permute-start(bf16[768,1024]{1,0:T(8,128)(2,1)S(1)} %bitcast.2), channel_id=1, source_target_pairs={{0,1},{1,0},{2,3},{3,2},{4,5},{5,4},{6,7},{7,6},{8,9},{9,8},{10,11... | collective-permute-start | bytes 4718600 | tf_op jit(solution)/shard_map/ppermute | solution.py:129

commit v4 on v3

--- a/solution.py
+++ b/solution.py
@@ -11,10 +11,10 @@
 
 sharpness = 3.0
 
+LATE_Z, LATE_XY = 10, 2
 AXES = ("zl", "y", "zh", "x", "c")
 SIZES = (8, 4, 2, 4, 2)
 Z = ("zh", "zl")
-PLANE = ("y", "x")
 NEAR = ("y", "x", "c")
 SWAP = [(0, 1), (1, 0)]
 WHOLE = pl.BlockSpec(memory_space=pltpu.VMEM)
@@ -30,13 +30,25 @@
     return pltpu.CompilerParams(vmem_limit_bytes=mib << 20)
 
 
-def exchange(copies, axes):
-    return lax.all_to_all(copies, axes, 0, 0, tiled=True)
+def line_groups(first):
+    at = np.arange(math.prod(SIZES)).reshape(SIZES)
+    lines = at.transpose(1, 3, 4, 2, 0).reshape(-1, count(Z))
+    return np.roll(lines, -first, axis=1).tolist()
 
 
-def spread(block, axes):
-    n = count(axes)
-    return exchange(lax.optimization_barrier(jnp.broadcast_to(block[None], (n,) + block.shape)), axes)
+def plane_groups(first, cores):
+    at = np.arange(math.prod(SIZES)).reshape(SIZES)
+    planes = at.transpose((0, 2, 1, 3, 4) if cores == 2 else (0, 2, 4, 1, 3)).reshape(-1, 4, 4, cores)
+    return np.roll(planes, (-first, -first), axis=(1, 2)).reshape(-1, 16 * cores).tolist()
+
+
+def exchange(copies, axes, groups=None):
+    return lax.all_to_all(copies, axes, 0, 0, tiled=True, axis_index_groups=groups)
+
+
+def spread(block, axes, groups=None):
+    n = len(groups[0]) if groups else count(axes)
+    return exchange(lax.optimization_barrier(jnp.broadcast_to(block[None], (n,) + block.shape)), axes, groups)
 
 
 def merge(parts):
@@ -124,12 +136,12 @@
     factor = sharpness / math.sqrt(width)
     own = texts[0]
     mass_scale = own.shape[0] / rows
-    line = spread(images.reshape(-1, 128), Z).reshape(-1, width)
-    mine = spread(line, PLANE).reshape(-1, width)
+    line = spread(images.reshape(-1, 128), AXES, line_groups(LATE_Z)).reshape(-1, width)
+    mine = spread(line, AXES, plane_groups(LATE_XY, 1)).reshape(-1, width)
     other = lax.ppermute(mine, "c", SWAP)
     shares_own, peak_own, lse = scores(own, mine, factor)
     shares_other, peak_other, lse = scores(own, other, factor, (lse,), count(NEAR))
-    parts = exchange(merged(exchange(lse, NEAR), count(Z)), Z)
+    parts = exchange(merged(exchange(lse, AXES, plane_groups(LATE_XY, 2)), count(Z)), AXES, line_groups(LATE_Z))
     return prototypes((shares_own, shares_other), parts, (peak_own, peak_other), (mine, other), mass_scale)
 
 

time: 101 us -> 92.5 us (0.916)
  blocking collectives: 81.8 us -> 76.7 us
  starting transfers between devices: 6.05 us -> 3.29 us
    all_to_all x4, blocking collectives: 81.8 us -> 76.7 us  [exchange(): lax.all_to_all(copies, axes, 0, 0, tiled=True, axis_index_groups=groups)]
    ppermute x1, starting transfers between devices: 6.05 us -> 3.29 us  [shards(): other = lax.ppermute(mine, 'c', SWAP)]
  transfers between devices with their start and end apart: 1 -> 1, of which waited for: 1 -> 1; matrix products, arithmetic and copies ran while one was open for 0% -> 0% of each run, Pallas kernels for 2% -> 3%
where the time goes in v4:
time: 92.5 us; the launch traced here: 92.2 us
  blocking collectives  76.7 us (83%)
  Pallas kernels  9.9 us (11%)
  starting transfers between devices  3.29 us (4%)
  local copies, waits for them, and re-layouts  0.97 us (1%)
    all_to_all x4, blocking collectives, exchange(): lax.all_to_all(copies, axes, 0, 0, tiled=True, axis_index_groups=groups)  76.7 us
    pallas_call x1, Pallas kernels, prototypes(): pl.pallas_call(functools.partial(prototypes_kernel, mass_scale), grid=(st...  4.84 us
    pallas_call x2, Pallas kernels, scores(): pl.pallas_call(functools.partial(scores_kernel, factor), out_shape=[struc...  4.82 us
    ppermute x1, starting transfers between devices, shards(): other = lax.ppermute(mine, 'c', SWAP)  3.29 us
  transfers between devices with their start and end apart: 1, of which 1 were waited for; matrix products, arithmetic and copies ran while one was open for 0% of the time, Pallas kernels for 3%

profile of v4, /device:TPU:1, one launch (start us, length us, event | category | flops | bytes accessed | tf_op | source)
XLA Modules:
  0.0 92.2 jit_solution(10179345383843887514)
XLA Ops:
  0.6 0.7 broadcast_in_dim.14
  1.4 23.5 %all_to_all.20 = bf16[16,24,128]{2,1,0:T(8,128)(2,1)S(1)} all-to-all(bf16[16,24,128]{2,1,0:T(8,128)(2,1)S(1)} %broadcast_in_dim.15), channel_id=1, replica_groups={{136,200,264,328,392,456,0,64,128,192,256,320,384,448,8,72},{137,201,26..., dimensions={0} | all-to-all | bytes 196608 | tf_op jit(solution)/shard_map/all_to_all | solution.py:46
  24.9 0.2 broadcast_in_dim.17
  25.1 0.0 copy-start
  25.1 25.9 %all_to_all.21 = bf16[16,48,1024]{2,1,0:T(8,128)(2,1)S(1)} all-to-all(bf16[16,48,1024]{2,1,0:T(8,128)(2,1)S(1)} %broadcast_in_dim.17), channel_id=1, replica_groups={{36,38,32,34,52,54,48,50,4,6,0,2,20,22,16,18},{37,39,33,35,53,55,49,51,..., dimensions={0} | all-to-all | bytes 3145728 | tf_op jit(solution)/shard_map/all_to_all | solution.py:46
  51.1 3.3 %collective-permute-start = (bf16[768,1024]{1,0:T(8,128)(2,1)S(1)}, bf16[768,1024]{1,0:T(8,128)(2,1)S(1)}, u32[]{:S(2)}, u32[]{:S(2)}) collective-permute-start(bf16[768,1024]{1,0:T(8,128)(2,1)S(1)} %bitcast.2), channel_id=1, source_target_pairs={{0,1},{1,0},{2,3},{3,2},{4,5},{5,4},{6,7},{7,6},{8,9},{9,8},{10,11... | collective-permute-start | bytes 4718600 | tf_op jit(solution)/shard_map/ppermute | solution.py:141
  54.4 0.0 copy-done
  54.4 2.4 %scores.2 = (bf16[1024,768]{1,0:T(8,128)(2,1)S(1)}, f32[1,768]{1,0:T(1,128)S(1)}, f32[1,768]{1,0:T(1,128)S(1)}) custom-call(bf16[1024,1024]{1,0:T(8,128)(2,1)S(1)} %bitcast.5, bf16[768,1024]{1,0:T(8,128)(2,1)S(1)} %bitcast.3), custom_call_target="tpu_custom_call" | custom-call | flops 1610612736 | bytes 5242880 | tf_op jit(solution)/shard_map/scores/pallas_call | solution.py:77
  56.8 0.6 collective-permute-done.images.images_other
  57.4 2.4 %scores.3 = (bf16[1024,768]{1,0:T(8,128)(2,1)S(1)}, f32[1,768]{1,0:T(1,128)S(1)}, f32[32,2,1,768]{3,2,1,0:T(1,128)S(1)}) custom-call(bf16[1024,1024]{1,0:T(8,128)(2,1)S(1)} %bitcast.6, bf16[768,1024]{1,0:T(8,128)(2,1)S(1)} %collective-permute-done.images.images_other, f32[1,768]{1,0:T(1,128)S(1)} %get-tuple-element.9.refs_0_), custom_call_target="tpu_custom_call" | custom-call | flops 1610612736 | bytes 5242880 | tf_op jit(solution)/shard_map/scores/pallas_call | solution.py:77
  59.8 10.9 %all_to_all.22.parts = f32[32,2,1,768]{3,2,1,0:T(1,128)S(1)} all-to-all(f32[32,2,1,768]{3,2,1,0:T(1,128)S(1)} %get-tuple-element.11), channel_id=1, replica_groups={{36,37,38,39,32,33,34,35,52,53,54,55,48,49,50,51,4,5,6,7,0,1,2,3,20,21,..., dimensions={0} | all-to-all | bytes 393216 | tf_op jit(solution)/shard_map/all_to_all | solution.py:46
  70.7 0.2 merge.1
  71.0 16.4 %all_to_all.23.parts = f32[16,2,1,768]{3,2,1,0:T(1,128)S(1)} all-to-all(f32[16,2,1,768]{3,2,1,0:T(1,128)S(1)} %merge.1), channel_id=1, replica_groups={{136,200,264,328,392,456,0,64,128,192,256,320,384,448,8,72},{137,201,26..., dimensions={0} | all-to-all | bytes 196608 | tf_op jit(solution)/shard_map/all_to_all | solution.py:46
  87.3 4.8 %prototypes.1 = (bf16[1,1024,1024]{2,1,0:T(8,128)(2,1)}, f32[1,1024]{1,0:T(1,128)}) custom-call(bf16[1024,768]{1,0:T(8,128)(2,1)S(1)} %get-tuple-element.8.shares_own, bf16[1024,768]{1,0:T(8,128)(2,1)S(1)} %get-tuple-element.10.shares_other, f32[16,2,1,768]{3,2,1,0:T(1,128)S(1)} %all_to_all.23.parts, f32[1,768]{1,0:T(1,128)S(1)} %get-tuple-element.12.peak_own, ...), custom_call_target="tpu_custom_call" | custom-call | flops 3221225472 | bytes 8388608 | tf_op jit(solution)/shard_map/prototypes/pallas_call | solution.py:122
  (2 shorter events, 0.1 us)
Async XLA Ops:
  25.1 29.3 %copy-start = (bf16[1,1024,1024]{2,1,0:T(8,128)(2,1)S(1)}, bf16[1,1024,1024]{2,1,0:T(8,128)(2,1)}, u32[]{:S(2)}) copy-start(bf16[1,1024,1024]{2,1,0:T(8,128)(2,1)} %param.3) | copy-start | bytes 6291460
  51.1 6.3 %collective-permute-start = (bf16[768,1024]{1,0:T(8,128)(2,1)S(1)}, bf16[768,1024]{1,0:T(8,128)(2,1)S(1)}, u32[]{:S(2)}, u32[]{:S(2)}) collective-permute-start(bf16[768,1024]{1,0:T(8,128)(2,1)S(1)} %bitcast.2), channel_id=1, source_target_pairs={{0,1},{1,0},{2,3},{3,2},{4,5},{5,4},{6,7},{7,6},{8,9},{9,8},{10,11... | collective-permute-start | bytes 4718600 | tf_op jit(solution)/shard_map/ppermute | solution.py:141

commit v5 on v4

--- a/solution.py
+++ b/solution.py
@@ -39,7 +39,7 @@
 def plane_groups(first, cores):
     at = np.arange(math.prod(SIZES)).reshape(SIZES)
     planes = at.transpose((0, 2, 1, 3, 4) if cores == 2 else (0, 2, 4, 1, 3)).reshape(-1, 4, 4, cores)
-    return np.roll(planes, (-first, -first), axis=(1, 2)).reshape(-1, 16 * cores).tolist()
+    return np.roll(planes, (-first, -first), axis=(1, 2))[..., ::-1].reshape(-1, 16 * cores).tolist()
 
 
 def exchange(copies, axes, groups=None):

time: 92.5 us -> 92.3 us (level)
  no operation moved by 1% of the time
where the time goes in v5:
time: 92.3 us; the launch traced here: 92 us
  blocking collectives  76.5 us (83%)
  Pallas kernels  9.9 us (11%)
  starting transfers between devices  3.29 us (4%)
  local copies, waits for them, and re-layouts  0.97 us (1%)
    all_to_all x4, blocking collectives, exchange(): lax.all_to_all(copies, axes, 0, 0, tiled=True, axis_index_groups=groups)  76.5 us
    pallas_call x1, Pallas kernels, prototypes(): pl.pallas_call(functools.partial(prototypes_kernel, mass_scale), grid=(st...  4.84 us
    pallas_call x2, Pallas kernels, scores(): pl.pallas_call(functools.partial(scores_kernel, factor), out_shape=[struc...  4.82 us
    ppermute x1, starting transfers between devices, shards(): other = lax.ppermute(mine, 'c', SWAP)  3.29 us
  transfers between devices with their start and end apart: 1, of which 1 were waited for; matrix products, arithmetic and copies ran while one was open for 0% of the time, Pallas kernels for 3%

profile of v5, /device:TPU:1, one launch (start us, length us, event | category | flops | bytes accessed | tf_op | source)
XLA Modules:
  0.0 92.0 jit_solution(17207992870335308913)
XLA Ops:
  0.6 0.7 broadcast_in_dim.14
  1.4 23.5 %all_to_all.20 = bf16[16,24,128]{2,1,0:T(8,128)(2,1)S(1)} all-to-all(bf16[16,24,128]{2,1,0:T(8,128)(2,1)S(1)} %broadcast_in_dim.15), channel_id=1, replica_groups={{136,200,264,328,392,456,0,64,128,192,256,320,384,448,8,72},{137,201,26..., dimensions={0} | all-to-all | bytes 196608 | tf_op jit(solution)/shard_map/all_to_all | solution.py:46
  24.9 0.2 broadcast_in_dim.17
  25.1 0.0 copy-start
  25.1 25.9 %all_to_all.21 = bf16[16,48,1024]{2,1,0:T(8,128)(2,1)S(1)} all-to-all(bf16[16,48,1024]{2,1,0:T(8,128)(2,1)S(1)} %broadcast_in_dim.17), channel_id=1, replica_groups={{36,38,32,34,52,54,48,50,4,6,0,2,20,22,16,18},{37,39,33,35,53,55,49,51,..., dimensions={0} | all-to-all | bytes 3145728 | tf_op jit(solution)/shard_map/all_to_all | solution.py:46
  51.1 3.3 %collective-permute-start = (bf16[768,1024]{1,0:T(8,128)(2,1)S(1)}, bf16[768,1024]{1,0:T(8,128)(2,1)S(1)}, u32[]{:S(2)}, u32[]{:S(2)}) collective-permute-start(bf16[768,1024]{1,0:T(8,128)(2,1)S(1)} %bitcast.2), channel_id=1, source_target_pairs={{0,1},{1,0},{2,3},{3,2},{4,5},{5,4},{6,7},{7,6},{8,9},{9,8},{10,11... | collective-permute-start | bytes 4718600 | tf_op jit(solution)/shard_map/ppermute | solution.py:141
  54.4 0.0 copy-done
  54.4 2.4 %scores.2 = (bf16[1024,768]{1,0:T(8,128)(2,1)S(1)}, f32[1,768]{1,0:T(1,128)S(1)}, f32[1,768]{1,0:T(1,128)S(1)}) custom-call(bf16[1024,1024]{1,0:T(8,128)(2,1)S(1)} %bitcast.5, bf16[768,1024]{1,0:T(8,128)(2,1)S(1)} %bitcast.3), custom_call_target="tpu_custom_call" | custom-call | flops 1610612736 | bytes 5242880 | tf_op jit(solution)/shard_map/scores/pallas_call | solution.py:77
  56.8 0.6 collective-permute-done.images.images_other
  57.4 2.4 %scores.3 = (bf16[1024,768]{1,0:T(8,128)(2,1)S(1)}, f32[1,768]{1,0:T(1,128)S(1)}, f32[32,2,1,768]{3,2,1,0:T(1,128)S(1)}) custom-call(bf16[1024,1024]{1,0:T(8,128)(2,1)S(1)} %bitcast.6, bf16[768,1024]{1,0:T(8,128)(2,1)S(1)} %collective-permute-done.images.images_other, f32[1,768]{1,0:T(1,128)S(1)} %get-tuple-element.9.refs_0_), custom_call_target="tpu_custom_call" | custom-call | flops 1610612736 | bytes 5242880 | tf_op jit(solution)/shard_map/scores/pallas_call | solution.py:77
  59.8 10.7 %all_to_all.22.parts = f32[32,2,1,768]{3,2,1,0:T(1,128)S(1)} all-to-all(f32[32,2,1,768]{3,2,1,0:T(1,128)S(1)} %get-tuple-element.11), channel_id=1, replica_groups={{37,36,39,38,33,32,35,34,53,52,55,54,49,48,51,50,5,4,7,6,1,0,3,2,21,20,..., dimensions={0} | all-to-all | bytes 393216 | tf_op jit(solution)/shard_map/all_to_all | solution.py:46
  70.5 0.2 merge.1
  70.8 16.4 %all_to_all.23.parts = f32[16,2,1,768]{3,2,1,0:T(1,128)S(1)} all-to-all(f32[16,2,1,768]{3,2,1,0:T(1,128)S(1)} %merge.1), channel_id=1, replica_groups={{136,200,264,328,392,456,0,64,128,192,256,320,384,448,8,72},{137,201,26..., dimensions={0} | all-to-all | bytes 196608 | tf_op jit(solution)/shard_map/all_to_all | solution.py:46
  87.1 4.8 %prototypes.1 = (bf16[1,1024,1024]{2,1,0:T(8,128)(2,1)}, f32[1,1024]{1,0:T(1,128)}) custom-call(bf16[1024,768]{1,0:T(8,128)(2,1)S(1)} %get-tuple-element.8.shares_own, bf16[1024,768]{1,0:T(8,128)(2,1)S(1)} %get-tuple-element.10.shares_other, f32[16,2,1,768]{3,2,1,0:T(1,128)S(1)} %all_to_all.23.parts, f32[1,768]{1,0:T(1,128)S(1)} %get-tuple-element.12.peak_own, ...), custom_call_target="tpu_custom_call" | custom-call | flops 3221225472 | bytes 8388608 | tf_op jit(solution)/shard_map/prototypes/pallas_call | solution.py:122
  (2 shorter events, 0.1 us)
Async XLA Ops:
  25.1 29.3 %copy-start = (bf16[1,1024,1024]{2,1,0:T(8,128)(2,1)S(1)}, bf16[1,1024,1024]{2,1,0:T(8,128)(2,1)}, u32[]{:S(2)}) copy-start(bf16[1,1024,1024]{2,1,0:T(8,128)(2,1)} %param.3) | copy-start | bytes 6291460
  51.1 6.3 %collective-permute-start = (bf16[768,1024]{1,0:T(8,128)(2,1)S(1)}, bf16[768,1024]{1,0:T(8,128)(2,1)S(1)}, u32[]{:S(2)}, u32[]{:S(2)}) collective-permute-start(bf16[768,1024]{1,0:T(8,128)(2,1)S(1)} %bitcast.2), channel_id=1, source_target_pairs={{0,1},{1,0},{2,3},{3,2},{4,5},{5,4},{6,7},{7,6},{8,9},{9,8},{10,11... | collective-permute-start | bytes 4718600 | tf_op jit(solution)/shard_map/ppermute | solution.py:141
